TPU v7x, 256 devices: a whole 4x4x8 slice. The times are simulated.
256 devices in a mesh: gx: 4 (over y_hi, core), gy: 4 (over x), gz: 16 (over y_lo, z).
Axes of the slice: x: 4, y: 4 (y_hi: 2, y_lo: 2; y = y_hi * 2 + y_lo), z: 8, core: 2. Of those that a mesh axis runs over, the one named last changes fastest.
Arguments:
- labels: int32 [32, 48, 2048], P('gx', 'gy', 'gz'), may hold values from 0 to 1
- density_jitter: float32 [2, 32, 48, 2048], P(None, 'gx', 'gy', 'gz'), may hold values from 0.7 to 1.4
- velocity: float32 [3, 32, 48, 2048], P(None, 'gx', 'gy', 'gz'), may hold values from -0.2 to 0.2
Outputs:
- populations: float32 [2, 19, 32, 48, 2048], P(None, None, 'gx', 'gy', 'gz')
All inputs are finite; a program needn't handle non-finite values.
Results may differ from a plain program's by a relative error of at most 0.0001.
Values sent between devices are 32-bit elements; how exact they have to be, the bound alone decides.
A program may use at most 192 MiB of HBM per device.

v0:
```python
import functools
import itertools

import jax
import jax.numpy as jnp
from jax import lax
from jax.experimental import pallas as pl
from jax.experimental.pallas import tpu as pltpu
from jax.sharding import PartitionSpec as P

MESH = pl.DeviceIdType.MESH
F32 = jnp.float32
VELS = [(0, 0, 0), (1, 0, 0), (-1, 0, 0), (0, 1, 0), (0, -1, 0), (0, 0, 1), (0, 0, -1),
        (1, 1, 0), (-1, -1, 0), (1, -1, 0), (-1, 1, 0), (1, 0, 1), (-1, 0, -1),
        (1, 0, -1), (-1, 0, 1), (0, 1, 1), (0, -1, -1), (0, 1, -1), (0, -1, 1)]
TAU_INV = (1.0, 1.25)
SRC = (0.5, 0.375)
GROUPS = [(a, b) for a in (-1, 0, 1) for b in (-1, 0, 1)]
ZGROUPS = [(0, 0), (1, 0), (-1, 0), (0, 1), (0, -1)]
NEIGHBOURS = [d for d in itertools.product((-1, 0, 1), repeat=3) if d != (0, 0, 0)]
EXCHANGED = [(2, 2, 48, 128), (3, 3, 32, 128), (2, 2, 2, 8, 128),
             (2, 2, 2, 40, 128), (2, 3, 3, 16, 128),
             (2, 2, 48, 128), (2, 3, 32, 128),
             (2, 2, 2, 40, 128), (2, 2, 3, 16, 128),
             (2, 3, 2, 2, 8, 128), (2, 3, 2, 2, 8, 128)]


def lane_of(rows):
    return lax.broadcasted_iota(jnp.int32, (rows, 128), 1)


def lroll(v, k):
    k = k % 128
    return v if isinstance(k, int) and k == 0 else pltpu.roll(v, k, 1)


def yroll(v, k):
    k = k % v.shape[0]
    return v if k == 0 else pltpu.roll(v, k, 0)


def z_place(f, x):
    if f < 2:
        return 0, 48 * f + 6 * x
    if f < 4:
        return 1, 48 * (f - 2) + 6 * x
    return (0, 96 + 6 * x) if x < 4 else (1, 96 + 6 * (x - 4))


def exchange_kernel(lab_ref, jit_ref, vel_ref, ro, uo, zp, rx, ux, ry, uy, re, ue, zf, ze,
                    labv, jitv, velv, lsem, ssem, rsem):
    ix, iy, iz = lax.axis_index("gx"), lax.axis_index("gy"), lax.axis_index("gz")
    nx, ny, nz = lax.axis_size("gx"), lax.axis_size("gy"), lax.axis_size("gz")

    def device(d):
        return (lax.rem(ix + d[0] + nx, nx), lax.rem(iy + d[1] + ny, ny), lax.rem(iz + d[2] + nz, nz))

    barrier = pltpu.get_barrier_semaphore()
    for d in NEIGHBOURS:
        pl.semaphore_signal(barrier, inc=1, device_id=device(d), device_id_type=MESH)
    loads = [pltpu.make_async_copy(a, b, lsem.at[n]) for n, (a, b) in
             enumerate(((lab_ref, labv), (jit_ref, jitv), (vel_ref, velv)))]
    for load in loads:
        load.start()
    for load in loads:
        load.wait()
    for x in range(8):
        drop = labv[x] == 1
        jitv[0, x] = jnp.where(drop, 2.0, 0.15).astype(F32) * jitv[0, x]
        jitv[1, x] = jnp.where(drop, 0.15, 2.0).astype(F32) * jitv[1, x]
    lane = lane_of(6)
    for h in range(2):
        packs = [[jnp.zeros((6, 128), F32) for _ in range(2)] for _ in range(2)]
        for f in range(5):
            for x in range(8):
                val = (jitv[f, x, 6 * h:6 * h + 6, :] if f < 2 else velv[f - 2, x, 6 * h:6 * h + 6, :])
                if f < 2:
                    ro[f, h, 6 * x:6 * x + 6, :] = val
                k, l0 = z_place(f, x)
                here = (lane >= l0) & (lane < l0 + 6)
                packs[0][k] = jnp.where(here, lroll(val, l0), packs[0][k])
                packs[1][k] = jnp.where(here, lroll(val, l0 + 6), packs[1][k])
        for zs in range(2):
            for k in range(2):
                zp[zs, h, k, 0:6, :] = packs[zs][k]
                zp[zs, h, k, 6:8, :] = packs[zs][k][0:2]
    for f in range(3):
        for g in range(3):
            for x in range(8):
                uo[f, g, 4 * x:4 * x + 4, :] = velv[f, x, 4 * g:4 * g + 4, :]
    pl.semaphore_wait(barrier, len(NEIGHBOURS))

    copies = []

    def send(src, dst, d):
        n = len(copies)
        copy = pltpu.make_async_remote_copy(src_ref=src, dst_ref=dst, send_sem=ssem.at[n], recv_sem=rsem.at[n],
                                            device_id=device(d), device_id_type=MESH)
        copy.start()
        copies.append(copy)

    for dz in (1, -1):
        zs_mine, zs_theirs = (1, 0) if dz == 1 else (0, 1)
        for dx in (0, 1, -1):
            send(zp.at[zs_mine], zf.at[zs_theirs, 1 - dx], (dx, 0, dz))
            for dy in (1, -1):
                h, side = (1, 0) if dy == 1 else (0, 1)
                send(zp.at[zs_mine, h], ze.at[zs_theirs, 1 - dx, side], (dx, dy, dz))
    for dx in (1, -1):
        sx, r0, u0 = (0, 8, 16) if dx == 1 else (1, 0, 0)
        send(ro.at[:, :, r0:r0 + 40], rx.at[sx], (dx, 0, 0))
        send(uo.at[:, :, u0:u0 + 16], ux.at[sx], (dx, 0, 0))
        for dy in (1, -1):
            sy, h, g = (0, 1, 2) if dy == 1 else (1, 0, 0)
            send(ro.at[:, h, r0:r0 + 40], re.at[sx, sy], (dx, dy, 0))
            send(uo.at[:, g, u0:u0 + 16], ue.at[sx, sy], (dx, dy, 0))
    for dy in (1, -1):
        sy, h, g = (0, 1, 2) if dy == 1 else (1, 0, 0)
        send(ro.at[:, h], ry.at[sy], (0, dy, 0))
        send(uo.at[:, g], uy.at[sy], (0, dy, 0))
    for copy in copies:
        copy.wait()


def exchange(labels, jitter, velocity):
    any_spec = pl.BlockSpec(memory_space=pl.ANY)
    vmem = pl.BlockSpec(memory_space=pltpu.VMEM)
    return pl.pallas_call(
        exchange_kernel,
        out_shape=[jax.ShapeDtypeStruct(s, F32) for s in EXCHANGED],
        in_specs=[any_spec] * 3,
        out_specs=[vmem] * len(EXCHANGED),
        scratch_shapes=[pltpu.VMEM((8, 12, 128), jnp.int32), pltpu.VMEM((2, 8, 12, 128), F32),
                        pltpu.VMEM((3, 8, 12, 128), F32), pltpu.SemaphoreType.DMA((3,)),
                        pltpu.SemaphoreType.DMA((34,)), pltpu.SemaphoreType.DMA((34,))],
        compiler_params=pltpu.CompilerParams(collective_id=0, has_side_effects=True, vmem_limit_bytes=16 << 20),
    )(labels, jitter, velocity)


NS1, NP1, NS2 = 34, 26, 28


def stage_a(src, slab, rho_is, fields):
    for s in range(2):
        p = 1.0 - jnp.exp(-src[s, slab])
        fields[s, 0, slab] = p
        for n, (k, c6, c12) in enumerate(((1, 0.25, 0.125), (2, 0.5 / 6, 0.5 / 12))):
            up, down = lroll(p, -k), lroll(p, k)
            bz = c6 * p + c12 * (up + down)
            dz = c12 * (up - down)
            fields[s, 1 + n, slab] = bz + c12 * (yroll(p, k) + yroll(p, -k))
            fields[s, 3 + n, slab] = bz
            fields[s, 5 + n, slab] = 2.0 * dz + (yroll(dz, k) + yroll(dz, -k))
            fields[s, 7 + n, slab] = dz


def force(fields, slab, rows):
    near, far = [], []
    for s in range(2):
        for n, (k, c12, out) in enumerate(((1, 0.125, near), (2, 0.5 / 12, far))):
            gx = fields[s, 1 + n, slab + k, 0:rows] - fields[s, 1 + n, slab - k, 0:rows]
            by = fields[s, 3 + n, slab] + c12 * (fields[s, 0, slab + k] + fields[s, 0, slab - k])
            gy = (yroll(by, -k) - yroll(by, k))[0:rows]
            gz = fields[s, 5 + n, slab, 0:rows] + (fields[s, 7 + n, slab + k, 0:rows] + fields[s, 7 + n, slab - k, 0:rows])
            out.append((gx, gy, gz))
    result = []
    for s in range(2):
        minus = -fields[s, 0, slab, 0:rows]
        result.append([minus * (near[1 - s][a] + far[s][a]) for a in range(3)])
    return result


def populations(s, rho, v, f, old=None):
    w = 1.0 / 36.0
    rt = (w * TAU_INV[s]) * rho
    vv = v[0] * v[0] + v[1] * v[1] + v[2] * v[2]
    vf = v[0] * f[0] + v[1] * f[1] + v[2] * f[2]
    a0 = rt * (1.0 - 1.5 * vv) - (3.0 * SRC[s] * w) * vf
    b = [3.0 * (rt * v[a] + (SRC[s] * w) * f[a]) for a in range(3)]
    g = [4.5 * rt * v[a] + (9.0 * SRC[s] * w) * f[a] for a in range(3)]
    diag = [v[a] * g[a] for a in range(3)]
    off = {(a, c): v[a] * g[c] + v[c] * g[a] for a, c in ((0, 1), (0, 2), (1, 2))}
    if old is not None:
        part = 1.0 - TAU_INV[s]
        ro = (w * part) * rho
        uu = old[0] * old[0] + old[1] * old[1] + old[2] * old[2]
        a0 = a0 + ro * (1.0 - 1.5 * uu)
        h = [4.5 * ro * old[a] for a in range(3)]
        b = [b[a] + 3.0 * ro * old[a] for a in range(3)]
        diag = [diag[a] + old[a] * h[a] for a in range(3)]
        off = {(a, c): off[a, c] + 2.0 * (old[a] * h[c]) for a, c in off}
    post = {(0, 0, 0): 12.0 * a0}
    for a in range(3):
        even, odd = a0 + diag[a], b[a]
        unit = [0, 0, 0]
        unit[a] = 1
        post[tuple(unit)] = 2.0 * (even + odd)
        post[tuple(-q for q in unit)] = 2.0 * (even - odd)
    for a, c in off:
        base = a0 + (diag[a] + diag[c])
        for sign in (1, -1):
            even = base + off[a, c] if sign == 1 else base - off[a, c]
            odd = b[a] + b[c] if sign == 1 else b[a] - b[c]
            unit = [0, 0, 0]
            unit[a], unit[c] = 1, sign
            post[tuple(unit)] = even + odd
            post[tuple(-q for q in unit)] = even - odd
    return post


def compute_kernel(ro, uo, zp, rx, ux, ry, uy, re, ue, zf, ze, out_ref,
                   rho, vel, zr, fld, pops, qs, qz, rho1, mom, fld1, sout, outx, sem):
    for e in range(20):
        dx, x = (0, e + 2) if e < 6 else (1, e - 6) if e < 14 else (2, e - 14)
        for c in range(2):
            for j in range(4):
                if dx == 1:
                    r0 = 6 * x
                    part = (ry[0, c, r0:r0 + 6] if j == 0 else ry[1, c, r0:r0 + 6] if j == 3 else
                            ro[c, j - 1, r0:r0 + 6])
                else:
                    sx = dx // 2
                    r0 = 6 * x - (8 if sx == 0 else 0)
                    part = (re[sx, 0, c, r0:r0 + 6] if j == 0 else re[sx, 1, c, r0:r0 + 6] if j == 3 else
                            rx[sx, c, j - 1, r0:r0 + 6])
                rho[c, e, 6 * j:6 * j + 6, :] = part
    for k in range(16):
        dx, x = (0, k + 4) if k < 4 else (1, k - 4) if k < 12 else (2, k - 12)
        for f in range(3):
            for j in range(5):
                if dx == 1:
                    r0 = 4 * x
                    part = (uy[0, f, r0:r0 + 4] if j == 0 else uy[1, f, r0:r0 + 4] if j == 4 else
                            uo[f, j - 1, r0:r0 + 4])
                else:
                    sx = dx // 2
                    r0 = 4 * x - (16 if sx == 0 else 0)
                    part = (ue[sx, 0, f, r0:r0 + 4] if j == 0 else ue[sx, 1, f, r0:r0 + 4] if j == 4 else
                            ux[sx, f, j - 1, r0:r0 + 4])
                vel[f, k, 2 + 4 * j:6 + 4 * j, :] = part
    for zs in range(2):
        for dx in range(3):
            for k in range(2):
                zr[zs, dx, k, 0:6] = ze[zs, dx, 0, k, 0:6]
                zr[zs, dx, k, 6:12] = zf[zs, dx, 0, k, 0:6]
                zr[zs, dx, k, 12:18] = zf[zs, dx, 1, k, 0:6]
                zr[zs, dx, k, 18:24] = ze[zs, dx, 1, k, 0:6]
    lane = lane_of(24)
    in_seg = lane % 18
    for f in range(5):
        merged = []
        for zs in range(2):
            m = jnp.zeros((24, 128), F32)
            for dx, (e_lo, e_hi) in enumerate(((0, 6), (6, 14), (14, 20))):
                off = 6 + 8 * (dx - 1)
                for x_lo, x_hi in ((0, 4), (4, 8)) if f == 4 else ((0, 8),):
                    a, b = max(e_lo, x_lo + off), min(e_hi, x_hi + off)
                    if a >= b:
                        continue
                    tile, l0 = z_place(f, x_lo)
                    shift = 6 * (x_lo + off) - l0
                    m = jnp.where((lane >= 6 * a) & (lane < 6 * b), lroll(zr[zs, dx, tile], shift), m)
            merged.append(m)
        for xo in range(3):
            low = lroll(merged[0], -6 * xo)
            high = lroll(merged[1], 6 - 6 * xo)
            for seg in range(7):
                e = 3 * seg + xo
                if f < 2:
                    if e > 19:
                        continue
                    val = rho[f, e]
                else:
                    if e < 2 or e > 17:
                        continue
                    val = vel[f - 2, e - 2]
                val = lroll(val, 18 * seg + 6)
                low = jnp.where((lane >= 18 * seg + 6) & (lane < 18 * seg + 18), val, low)
                start = (18 * seg - 6) % 128
                if seg == 0:
                    high = jnp.where((lane >= 122) | (lane < 6), val, high)
                else:
                    high = jnp.where((lane >= start) & (lane < start + 12), val, high)
            if f < 2:
                for base, v in ((20, low), (27, high)):
                    rho[f, base + 2 + xo] = v
                    if xo == 0:
                        rho[f, base + 5] = lroll(v, -18)
                    if xo == 1:
                        rho[f, base] = lroll(v, 18)
                        rho[f, base + 6] = lroll(v, -18)
                    if xo == 2:
                        rho[f, base + 1] = lroll(v, 18)
            else:
                vel[f - 2, 16 + xo] = low
                vel[f - 2, 19 + xo] = high

    @pl.loop(0, NS1)
    def _(slab):
        stage_a(rho, slab, None, fld)

    @pl.loop(0, 22)
    def _(j):
        late, later = (j >= 16).astype(jnp.int32), (j >= 19).astype(jnp.int32)
        slab = j + 2 + 4 * late + 4 * later
        dst = j + late + 2 * later
        fs = force(fld, slab, 24)
        r = [rho[s, slab] for s in range(2)]
        u = [vel[a, j] for a in range(3)]
        half = 0.5 / (r[0] + r[1])
        v = [u[a] + half * (fs[0][a] + fs[1][a]) for a in range(3)]
        zsum = {}
        for s in range(2):
            post = populations(s, r[s], v, fs[s], u if s == 1 else None)
            sums = {}
            for i, (cx, cy, cz) in enumerate(VELS):
                val = lroll(post[VELS[i]], cz)
                if s == 1:
                    pops[i, dst, 8:32] = val
                sums[cx, cy] = val if (cx, cy) not in sums else sums[cx, cy] + val
                if cz:
                    part = val if cz == 1 else -val
                    zsum[cx, cy] = part if (cx, cy) not in zsum else zsum[cx, cy] + part
            for n, key in enumerate(GROUPS):
                qs[s, n, dst, 8:32] = sums[key]
        for n, key in enumerate(ZGROUPS):
            qz[n, dst, 8:32] = zsum[key]

    for base in (16, 21):
        for n, (cx, cy) in enumerate(GROUPS):
            for s in range(2):
                if cx == 1:
                    qs[s, n, base, 8:32] = lroll(qs[s, n, base + 3, 8:32], 18)
                if cx == -1:
                    qs[s, n, base + 4, 8:32] = lroll(qs[s, n, base + 1, 8:32], -18)
        for n, (cx, cy) in enumerate(ZGROUPS):
            if cx == 1:
                qz[n, base, 8:32] = lroll(qz[n, base + 3, 8:32], 18)
            if cx == -1:
                qz[n, base + 4, 8:32] = lroll(qz[n, base + 1, 8:32], -18)
        for i, (cx, cy, cz) in enumerate(VELS):
            if cx == 1:
                pops[i, base, 8:32] = lroll(pops[i, base + 3, 8:32], 18)
            if cx == -1:
                pops[i, base + 4, 8:32] = lroll(pops[i, base + 1, 8:32], -18)

    @pl.loop(0, 20)
    def _(g):
        late, later = (g >= 14).astype(jnp.int32), (g >= 17).astype(jnp.int32)
        src = g + 1 + 2 * late + 2 * later
        dst = g + 2 * late + 4 * later
        mx = my = 0.0
        for s in range(2):
            top = bottom = 0.0
            for n, (cx, cy) in enumerate(GROUPS):
                a = qs[s, n, src - cx, 13 - cy:29 - cy]
                top = top + a
                bottom = bottom + qs[s, n, src - cx, 5 - cy:13 - cy]
                mx = mx + cx * a if cx else mx
                my = my + cy * a if cy else my
            rho1[s, dst, 0:16] = top
            rho1[s, dst, 16:24] = bottom
        mz = 0.0
        for n, (cx, cy) in enumerate(ZGROUPS):
            mz = mz + qz[n, src - cx, 13 - cy:29 - cy]
        mom[0, dst], mom[1, dst], mom[2, dst] = mx, my, mz

    for base in (14, 21):
        for s in range(2):
            rho1[s, base] = lroll(rho1[s, base + 3], 18)
            rho1[s, base + 1] = lroll(rho1[s, base + 4], 18)
            rho1[s, base + 5] = lroll(rho1[s, base + 2], -18)
            rho1[s, base + 6] = lroll(rho1[s, base + 3], -18)

    @pl.loop(0, NS2)
    def _(slab):
        stage_a(rho1, slab, None, fld1)

    def second(slab, src, write):
        fs = force(fld1, slab, 16)
        r = [rho1[s, slab, 0:16] for s in range(2)]
        inv = 1.0 / (r[0] + r[1])
        v = [(mom[a, slab] + 0.5 * (fs[0][a] + fs[1][a])) * inv for a in range(3)]
        for s in range(2):
            post = populations(s, r[s], v, fs[s])
            for i, (cx, cy, cz) in enumerate(VELS):
                val = post[VELS[i]]
                if s == 1:
                    val = val - 0.25 * pops[i, src - cx, 13 - cy:29 - cy]
                write(s, i, yroll(lroll(val, cz), cy - 1))

    @pl.loop(0, 6)
    def _(t):
        later = (t >= 3).astype(jnp.int32)

        def write(s, i, val):
            sout[s, i, t] = val

        second(16 + t + 4 * later, 17 + t + 2 * later, write)

    lane16 = lane_of(16)
    seg16 = lane16 % 18
    from_low = (seg16 >= 6) & (seg16 < 12)
    edge = (lane16 < 6) | (lane16 >= 122)

    @pl.loop(0, 10)
    def _(k):
        e = k + 5
        seg = e // 3
        xo = e - 3 * seg
        shift = lax.rem(256 - 18 * seg - 6, 128)

        def write(s, i, val):
            cx = VELS[i][0]
            strip = jnp.where(from_low, sout[s, i, xo], sout[s, i, xo + 3])
            val = jnp.where(edge, pltpu.roll(strip, shift, 1), val)
            outx[s, i, k + 1 + cx] = val[0:12]

        second(k + 2, k + 3, write)

    copy = pltpu.make_async_copy(outx.at[:, :, 2:10], out_ref, sem.at[0])
    copy.start()
    copy.wait()


def compute(parts):
    vmem = pl.BlockSpec(memory_space=pltpu.VMEM)
    return pl.pallas_call(
        compute_kernel,
        out_shape=jax.ShapeDtypeStruct((2, 19, 8, 12, 128), F32),
        in_specs=[vmem] * len(parts),
        out_specs=pl.BlockSpec(memory_space=pl.ANY),
        scratch_shapes=[
            pltpu.VMEM((2, NS1, 24, 128), F32), pltpu.VMEM((3, 22, 24, 128), F32), pltpu.VMEM((2, 3, 2, 24, 128), F32),
            pltpu.VMEM((2, 9, NS1, 24, 128), F32), pltpu.VMEM((19, NP1, 40, 128), F32),
            pltpu.VMEM((2, 9, NP1, 40, 128), F32), pltpu.VMEM((5, NP1, 40, 128), F32),
            pltpu.VMEM((2, NS2, 24, 128), F32), pltpu.VMEM((3, NS2, 16, 128), F32),
            pltpu.VMEM((2, 9, NS2, 24, 128), F32), pltpu.VMEM((2, 19, 6, 16, 128), F32),
            pltpu.VMEM((2, 19, 12, 12, 128), F32), pltpu.SemaphoreType.DMA((1,))],
        compiler_params=pltpu.CompilerParams(vmem_limit_bytes=58 << 20),
    )(*parts)


def local(labels, density_jitter, velocity):
    return compute(exchange(labels, density_jitter, velocity))


def solution(mesh):
    in_specs = (P("gx", "gy", "gz"), P(None, "gx", "gy", "gz"), P(None, "gx", "gy", "gz"))
    out_specs = P(None, None, "gx", "gy", "gz")
    return jax.shard_map(local, mesh=mesh, in_specs=in_specs, out_specs=out_specs, check_vma=False)
```

profile of v0, /device:TPU:1, one launch (start us, length us, event | category | flops | bytes accessed | tf_op | source)
XLA Modules:
  0.0 54.8 jit_solution(6721985914115664339)
XLA Ops:
  0.0 0.8 %copy.4.lab_ref = s32[8,12,128]{2,1,0:T(8,128)S(1)} copy(s32[8,12,128]{2,0,1:T(8,128)} %param.3) | data formatting | bytes 98304 | tf_op args[0]
  0.8 0.9 %copy.5.jit_ref = f32[2,8,12,128]{3,2,1,0:T(8,128)S(1)} copy(f32[2,8,12,128]{3,1,2,0:T(8,128)} %param.4) | data formatting | bytes 196608 | tf_op args[1]
  1.7 0.9 %copy.6.vel_ref = f32[3,8,12,128]{3,2,1,0:T(8,128)S(1)} copy(f32[3,8,12,128]{3,1,2,0:T(8,128)} %param.5) | data formatting | bytes 294912 | tf_op args[2]
  2.7 22.2 %shard_map.37 = (f32[2,2,48,128]{3,2,1,0:T(8,128)S(1)}, f32[3,3,32,128]{3,2,1,0:T(8,128)S(1)}, f32[2,2,2,8,128]{4,3,2,1,0:T(8,128)S(1)}, f32[2,2,2,40,128]{4,3,2...) custom-call(s32[8,12,128]{2,1,0:T(8,128)S(1)} %copy.4.lab_ref, ...), custom_call_target="tpu_custom_call" | custom-call | tf_op jit(solution)/shard_map/pallas_call | solution.py:128
  24.9 0.0 copy-start
  24.9 0.7 %copy-done = f32[2,2,2,40,128]{4,3,2,1,0:T(8,128)} copy-done((f32[2,2,2,40,128]{4,3,2,1,0:T(8,128)}, f32[2,2,2,40,128]{4,3,2,1,0:T(8,128)S(1)}, u32[]{:S(2)}) %copy-start) | copy-done | bytes 163864
  25.5 0.0 copy-start.1
  25.5 0.7 %copy-done.1 = f32[2,2,2,40,128]{4,3,2,1,0:T(8,128)} copy-done((f32[2,2,2,40,128]{4,3,2,1,0:T(8,128)}, f32[2,2,2,40,128]{4,3,2,1,0:T(8,128)S(1)}, u32[]{:S(2)}) %copy-start.1) | copy-done | bytes 163864
  26.2 0.0 copy-start.2
  26.2 0.7 %copy-done.2 = f32[3,3,32,128]{3,2,1,0:T(8,128)} copy-done((f32[3,3,32,128]{3,2,1,0:T(8,128)}, f32[3,3,32,128]{3,2,1,0:T(8,128)S(1)}, u32[]{:S(2)}) %copy-start.2) | copy-done | bytes 147480
  26.8 0.0 copy-start.3
  26.8 0.7 %copy-done.3 = f32[2,3,3,16,128]{4,3,2,1,0:T(8,128)} copy-done((f32[2,3,3,16,128]{4,3,2,1,0:T(8,128)}, f32[2,3,3,16,128]{4,3,2,1,0:T(8,128)S(1)}, u32[]{:S(2)}) %copy-start.3) | copy-done | bytes 147480
  27.5 0.0 copy-start.4
  27.5 0.6 %copy-done.4 = f32[2,2,48,128]{3,2,1,0:T(8,128)} copy-done((f32[2,2,48,128]{3,2,1,0:T(8,128)}, f32[2,2,48,128]{3,2,1,0:T(8,128)S(1)}, u32[]{:S(2)}) %copy-start.4) | copy-done | bytes 98328
  28.1 0.0 copy-start.5
  28.1 0.6 %copy-done.5 = f32[2,2,48,128]{3,2,1,0:T(8,128)} copy-done((f32[2,2,48,128]{3,2,1,0:T(8,128)}, f32[2,2,48,128]{3,2,1,0:T(8,128)S(1)}, u32[]{:S(2)}) %copy-start.5) | copy-done | bytes 98328
  28.8 0.0 copy-start.6
  28.8 0.6 %copy-done.6 = f32[2,3,32,128]{3,2,1,0:T(8,128)} copy-done((f32[2,3,32,128]{3,2,1,0:T(8,128)}, f32[2,3,32,128]{3,2,1,0:T(8,128)S(1)}, u32[]{:S(2)}) %copy-start.6) | copy-done | bytes 98328
  29.4 0.0 copy-start.7
  29.4 0.6 %copy-done.7 = f32[2,2,3,16,128]{4,3,2,1,0:T(8,128)} copy-done((f32[2,2,3,16,128]{4,3,2,1,0:T(8,128)}, f32[2,2,3,16,128]{4,3,2,1,0:T(8,128)S(1)}, u32[]{:S(2)}) %copy-start.7) | copy-done | bytes 98328
  30.1 0.0 copy-start.8
  30.1 0.6 %copy-done.8 = f32[2,3,2,2,8,128]{5,4,3,2,1,0:T(8,128)} copy-done((f32[2,3,2,2,8,128]{5,4,3,2,1,0:T(8,128)}, f32[2,3,2,2,8,128]{5,4,3,2,1,0:T(8,128)S(1)}, u32[]{:S(2)}) %copy-start.8) | copy-done | bytes 98328
  30.7 0.0 copy-start.9
  30.7 0.6 %copy-done.9 = f32[2,3,2,2,8,128]{5,4,3,2,1,0:T(8,128)} copy-done((f32[2,3,2,2,8,128]{5,4,3,2,1,0:T(8,128)}, f32[2,3,2,2,8,128]{5,4,3,2,1,0:T(8,128)S(1)}, u32[]{:S(2)}) %copy-start.9) | copy-done | bytes 98328
  31.3 0.0 copy-start.10
  31.3 0.6 %copy-done.10 = f32[2,2,2,8,128]{4,3,2,1,0:T(8,128)} copy-done((f32[2,2,2,8,128]{4,3,2,1,0:T(8,128)}, f32[2,2,2,8,128]{4,3,2,1,0:T(8,128)S(1)}, u32[]{:S(2)}) %copy-start.10) | copy-done | bytes 32792
  31.9 19.1 %shard_map.38 = f32[2,19,8,12,128]{4,3,2,1,0:T(8,128)} custom-call(f32[2,2,48,128]{3,2,1,0:T(8,128)} %copy-done.4, f32[3,3,32,128]{3,2,1,0:T(8,128)} %copy-done.2, f32[2,2,2,8,128]{4,3,2,1,0:T(8,128)} %copy-done.10, f32[2,2,2,40,128]{4,3,2,1,0:T(8,128)} %copy-done, f32[2,3,3,16,128]{4,3,2,1,0:T(8,128)} %copy-done.3, f32[2,2,48,128]{3,2,1,0:T(8,128)} %copy-done.5, ...), custom_call_target="tpu_custom_call" | custom-call | tf_op jit(solution)/shard_map/pallas_call | solution.py:428
  51.0 3.8 %copy.7 = f32[2,19,8,12,128]{4,2,3,1,0:T(8,128)} copy(f32[2,19,8,12,128]{4,3,2,1,0:T(8,128)} %shard_map.38) | data formatting | bytes 3735552 | tf_op jit(solution)/shard_map/pallas_call | solution.py:428
Async XLA Ops:
  24.9 0.7 %copy-start = (f32[2,2,2,40,128]{4,3,2,1,0:T(8,128)}, f32[2,2,2,40,128]{4,3,2,1,0:T(8,128)S(1)}, u32[]{:S(2)}) copy-start(f32[2,2,2,40,128]{4,3,2,1,0:T(8,128)S(1)} %get-tuple-element.19.rx) | copy-start | bytes 491524
  25.5 0.7 %copy-start.1 = (f32[2,2,2,40,128]{4,3,2,1,0:T(8,128)}, f32[2,2,2,40,128]{4,3,2,1,0:T(8,128)S(1)}, u32[]{:S(2)}) copy-start(f32[2,2,2,40,128]{4,3,2,1,0:T(8,128)S(1)} %get-tuple-element.23.re) | copy-start | bytes 491524
  26.2 0.7 %copy-start.2 = (f32[3,3,32,128]{3,2,1,0:T(8,128)}, f32[3,3,32,128]{3,2,1,0:T(8,128)S(1)}, u32[]{:S(2)}) copy-start(f32[3,3,32,128]{3,2,1,0:T(8,128)S(1)} %get-tuple-element.17.uo) | copy-start | bytes 442372
  26.8 0.7 %copy-start.3 = (f32[2,3,3,16,128]{4,3,2,1,0:T(8,128)}, f32[2,3,3,16,128]{4,3,2,1,0:T(8,128)S(1)}, u32[]{:S(2)}) copy-start(f32[2,3,3,16,128]{4,3,2,1,0:T(8,128)S(1)} %get-tuple-element.20.ux) | copy-start | bytes 442372
  27.5 0.6 %copy-start.4 = (f32[2,2,48,128]{3,2,1,0:T(8,128)}, f32[2,2,48,128]{3,2,1,0:T(8,128)S(1)}, u32[]{:S(2)}) copy-start(f32[2,2,48,128]{3,2,1,0:T(8,128)S(1)} %get-tuple-element.16.ro) | copy-start | bytes 294916
  28.1 0.6 %copy-start.5 = (f32[2,2,48,128]{3,2,1,0:T(8,128)}, f32[2,2,48,128]{3,2,1,0:T(8,128)S(1)}, u32[]{:S(2)}) copy-start(f32[2,2,48,128]{3,2,1,0:T(8,128)S(1)} %get-tuple-element.21.ry) | copy-start | bytes 294916
  28.8 0.6 %copy-start.6 = (f32[2,3,32,128]{3,2,1,0:T(8,128)}, f32[2,3,32,128]{3,2,1,0:T(8,128)S(1)}, u32[]{:S(2)}) copy-start(f32[2,3,32,128]{3,2,1,0:T(8,128)S(1)} %get-tuple-element.22.uy) | copy-start | bytes 294916
  29.4 0.6 %copy-start.7 = (f32[2,2,3,16,128]{4,3,2,1,0:T(8,128)}, f32[2,2,3,16,128]{4,3,2,1,0:T(8,128)S(1)}, u32[]{:S(2)}) copy-start(f32[2,2,3,16,128]{4,3,2,1,0:T(8,128)S(1)} %get-tuple-element.24.ue) | copy-start | bytes 294916
  30.1 0.6 %copy-start.8 = (f32[2,3,2,2,8,128]{5,4,3,2,1,0:T(8,128)}, f32[2,3,2,2,8,128]{5,4,3,2,1,0:T(8,128)S(1)}, u32[]{:S(2)}) copy-start(f32[2,3,2,2,8,128]{5,4,3,2,1,0:T(8,128)S(1)} %get-tuple-element.25.zf) | copy-start | bytes 294916
  30.7 0.6 %copy-start.9 = (f32[2,3,2,2,8,128]{5,4,3,2,1,0:T(8,128)}, f32[2,3,2,2,8,128]{5,4,3,2,1,0:T(8,128)S(1)}, u32[]{:S(2)}) copy-start(f32[2,3,2,2,8,128]{5,4,3,2,1,0:T(8,128)S(1)} %get-tuple-element.26.ze) | copy-start | bytes 294916
  31.3 0.6 %copy-start.10 = (f32[2,2,2,8,128]{4,3,2,1,0:T(8,128)}, f32[2,2,2,8,128]{4,3,2,1,0:T(8,128)S(1)}, u32[]{:S(2)}) copy-start(f32[2,2,2,8,128]{4,3,2,1,0:T(8,128)S(1)} %get-tuple-element.18.zp) | copy-start | bytes 98308
where the time goes:
time: 55 us; the launch traced here: 54.8 us
  Pallas kernels  41.3 us (75%)
  local copies, waits for them, and re-layouts  13.5 us (25%)
    pallas_call x1, Pallas kernels, exchange(): pl.pallas_call(exchange_kernel, out_shape=[jax.ShapeDtypeStruct(s, F32) f...  22.2 us
    pallas_call x1, Pallas kernels, compute(): pl.pallas_call(compute_kernel, out_shape=jax.ShapeDtypeStruct((2, 19, 8,...  19.1 us
    unnamed x25, local copies, waits for them, and re-layouts  9.71 us
    pallas_call x1, local copies, waits for them, and re-layouts, compute(): pl.pallas_call(compute_kernel, out_shape=jax.ShapeDtypeStruct((2, 19, 8,...  3.75 us

commit v1 on v0

--- a/solution.py
+++ b/solution.py
@@ -48,7 +48,7 @@
 
 
 def exchange_kernel(lab_ref, jit_ref, vel_ref, ro, uo, zp, rx, ux, ry, uy, re, ue, zf, ze,
-                    labv, jitv, velv, lsem, ssem, rsem):
+                    labv, jitv, velv, lsem, ssem, rsem, below):
     ix, iy, iz = lax.axis_index("gx"), lax.axis_index("gy"), lax.axis_index("gz")
     nx, ny, nz = lax.axis_size("gx"), lax.axis_size("gy"), lax.axis_size("gz")
 
@@ -57,23 +57,24 @@
 
     barrier = pltpu.get_barrier_semaphore()
     for d in NEIGHBOURS:
-        pl.semaphore_signal(barrier, inc=1, device_id=device(d), device_id_type=MESH)
+        if d[2] <= 0:
+            pl.semaphore_signal(barrier, inc=1, device_id=device(d), device_id_type=MESH)
     loads = [pltpu.make_async_copy(a, b, lsem.at[n]) for n, (a, b) in
              enumerate(((lab_ref, labv), (jit_ref, jitv), (vel_ref, velv)))]
     for load in loads:
         load.start()
     for load in loads:
         load.wait()
-    for x in range(8):
-        drop = labv[x] == 1
-        jitv[0, x] = jnp.where(drop, 2.0, 0.15).astype(F32) * jitv[0, x]
-        jitv[1, x] = jnp.where(drop, 0.15, 2.0).astype(F32) * jitv[1, x]
+    drop = labv[...] == 1
+    jitv[0] = jnp.where(drop, 2.0, 0.15).astype(F32) * jitv[0]
+    jitv[1] = jnp.where(drop, 0.15, 2.0).astype(F32) * jitv[1]
     lane = lane_of(6)
     for h in range(2):
         packs = [[jnp.zeros((6, 128), F32) for _ in range(2)] for _ in range(2)]
         for f in range(5):
             for x in range(8):
-                val = (jitv[f, x, 6 * h:6 * h + 6, :] if f < 2 else velv[f - 2, x, 6 * h:6 * h + 6, :])
+                rows = pl.ds(48 * h + x, 6, stride=8)
+                val = jitv[f, rows, :] if f < 2 else velv[f - 2, rows, :]
                 if f < 2:
                     ro[f, h, 6 * x:6 * x + 6, :] = val
                 k, l0 = z_place(f, x)
@@ -87,8 +88,11 @@
     for f in range(3):
         for g in range(3):
             for x in range(8):
-                uo[f, g, 4 * x:4 * x + 4, :] = velv[f, x, 4 * g:4 * g + 4, :]
-    pl.semaphore_wait(barrier, len(NEIGHBOURS))
+                uo[f, g, 4 * x:4 * x + 4, :] = velv[f, pl.ds(32 * g + x, 4, stride=8), :]
+    pl.semaphore_wait(barrier, 17)
+    for d in NEIGHBOURS:
+        if d[2] == 1:
+            pl.semaphore_signal(below, inc=1, device_id=device(d), device_id_type=MESH)
 
     copies = []
 
@@ -99,13 +103,15 @@
         copy.start()
         copies.append(copy)
 
-    for dz in (1, -1):
+    def send_z(dz):
         zs_mine, zs_theirs = (1, 0) if dz == 1 else (0, 1)
         for dx in (0, 1, -1):
             send(zp.at[zs_mine], zf.at[zs_theirs, 1 - dx], (dx, 0, dz))
             for dy in (1, -1):
                 h, side = (1, 0) if dy == 1 else (0, 1)
                 send(zp.at[zs_mine, h], ze.at[zs_theirs, 1 - dx, side], (dx, dy, dz))
+
+    send_z(1)
     for dx in (1, -1):
         sx, r0, u0 = (0, 8, 16) if dx == 1 else (1, 0, 0)
         send(ro.at[:, :, r0:r0 + 40], rx.at[sx], (dx, 0, 0))
@@ -118,22 +124,24 @@
         sy, h, g = (0, 1, 2) if dy == 1 else (1, 0, 0)
         send(ro.at[:, h], ry.at[sy], (0, dy, 0))
         send(uo.at[:, g], uy.at[sy], (0, dy, 0))
+    pl.semaphore_wait(below, 9)
+    send_z(-1)
     for copy in copies:
         copy.wait()
 
 
 def exchange(labels, jitter, velocity):
-    any_spec = pl.BlockSpec(memory_space=pl.ANY)
+    hbm = pl.BlockSpec(memory_space=pltpu.HBM)
     vmem = pl.BlockSpec(memory_space=pltpu.VMEM)
     return pl.pallas_call(
         exchange_kernel,
         out_shape=[jax.ShapeDtypeStruct(s, F32) for s in EXCHANGED],
-        in_specs=[any_spec] * 3,
+        in_specs=[hbm] * 3,
         out_specs=[vmem] * len(EXCHANGED),
-        scratch_shapes=[pltpu.VMEM((8, 12, 128), jnp.int32), pltpu.VMEM((2, 8, 12, 128), F32),
-                        pltpu.VMEM((3, 8, 12, 128), F32), pltpu.SemaphoreType.DMA((3,)),
-                        pltpu.SemaphoreType.DMA((34,)), pltpu.SemaphoreType.DMA((34,))],
-        compiler_params=pltpu.CompilerParams(collective_id=0, has_side_effects=True, vmem_limit_bytes=16 << 20),
+        scratch_shapes=[pltpu.VMEM((96, 128), jnp.int32), pltpu.VMEM((2, 96, 128), F32),
+                        pltpu.VMEM((3, 96, 128), F32), pltpu.SemaphoreType.DMA((3,)),
+                        pltpu.SemaphoreType.DMA((34,)), pltpu.SemaphoreType.DMA((34,)), pltpu.SemaphoreType.REGULAR],
+        compiler_params=pltpu.CompilerParams(collective_id=0, has_side_effects=True, vmem_limit_bytes=8 << 20),
     )(labels, jitter, velocity)
 
 
@@ -209,7 +217,7 @@
 
 
 def compute_kernel(ro, uo, zp, rx, ux, ry, uy, re, ue, zf, ze, out_ref,
-                   rho, vel, zr, fld, pops, qs, qz, rho1, mom, fld1, sout, outx, sem):
+                   rho, vel, zr, fld, pops, qs, qz, rho1, mom, sout, outx, sem):
     for e in range(20):
         dx, x = (0, e + 2) if e < 6 else (1, e - 6) if e < 14 else (2, e - 14)
         for c in range(2):
@@ -374,10 +382,10 @@
 
     @pl.loop(0, NS2)
     def _(slab):
-        stage_a(rho1, slab, None, fld1)
+        stage_a(rho1, slab, None, fld)
 
     def second(slab, src, write):
-        fs = force(fld1, slab, 16)
+        fs = force(fld, slab, 16)
         r = [rho1[s, slab, 0:16] for s in range(2)]
         inv = 1.0 / (r[0] + r[1])
         v = [(mom[a, slab] + 0.5 * (fs[0][a] + fs[1][a])) * inv for a in range(3)]
@@ -414,11 +422,13 @@
             cx = VELS[i][0]
             strip = jnp.where(from_low, sout[s, i, xo], sout[s, i, xo + 3])
             val = jnp.where(edge, pltpu.roll(strip, shift, 1), val)
-            outx[s, i, k + 1 + cx] = val[0:12]
+            x = k - 1 + cx
+            inside = (x >= 0) & (x < 8)
+            outx[s, i, pl.ds(jnp.where(inside, x, 96), 12, stride=8)] = val[0:12]
 
         second(k + 2, k + 3, write)
 
-    copy = pltpu.make_async_copy(outx.at[:, :, 2:10], out_ref, sem.at[0])
+    copy = pltpu.make_async_copy(outx.at[:, :, 0:96], out_ref, sem.at[0])
     copy.start()
     copy.wait()
 
@@ -427,22 +437,24 @@
     vmem = pl.BlockSpec(memory_space=pltpu.VMEM)
     return pl.pallas_call(
         compute_kernel,
-        out_shape=jax.ShapeDtypeStruct((2, 19, 8, 12, 128), F32),
+        out_shape=jax.ShapeDtypeStruct((2, 19, 96, 128), F32),
         in_specs=[vmem] * len(parts),
-        out_specs=pl.BlockSpec(memory_space=pl.ANY),
+        out_specs=pl.BlockSpec(memory_space=pltpu.HBM),
         scratch_shapes=[
             pltpu.VMEM((2, NS1, 24, 128), F32), pltpu.VMEM((3, 22, 24, 128), F32), pltpu.VMEM((2, 3, 2, 24, 128), F32),
             pltpu.VMEM((2, 9, NS1, 24, 128), F32), pltpu.VMEM((19, NP1, 40, 128), F32),
             pltpu.VMEM((2, 9, NP1, 40, 128), F32), pltpu.VMEM((5, NP1, 40, 128), F32),
             pltpu.VMEM((2, NS2, 24, 128), F32), pltpu.VMEM((3, NS2, 16, 128), F32),
-            pltpu.VMEM((2, 9, NS2, 24, 128), F32), pltpu.VMEM((2, 19, 6, 16, 128), F32),
-            pltpu.VMEM((2, 19, 12, 12, 128), F32), pltpu.SemaphoreType.DMA((1,))],
-        compiler_params=pltpu.CompilerParams(vmem_limit_bytes=58 << 20),
+            pltpu.VMEM((2, 19, 6, 16, 128), F32),
+            pltpu.VMEM((2, 19, 192, 128), F32), pltpu.SemaphoreType.DMA((1,))],
+        compiler_params=pltpu.CompilerParams(vmem_limit_bytes=40 << 20),
     )(*parts)
 
 
 def local(labels, density_jitter, velocity):
-    return compute(exchange(labels, density_jitter, velocity))
+    rows = [jnp.swapaxes(a, -3, -2).reshape(a.shape[:-3] + (96, 128)) for a in (labels, density_jitter, velocity)]
+    out = compute(exchange(*rows))
+    return jnp.swapaxes(out.reshape(2, 19, 12, 8, 128), 2, 3)
 
 
 def solution(mesh):

time: 55 us -> 39.4 us (0.72)
  local copies, waits for them, and re-layouts: 13.5 us -> 2.6 us
  Pallas kernels: 41.3 us -> 36 us
    unnamed x25 -> x6, local copies, waits for them, and re-layouts: 9.71 us -> 2.6 us
    pallas_call x1, Pallas kernels: 22.2 us -> 18.2 us  [exchange(): pl.pallas_call(exchange_kernel, out_shape=[jax.ShapeDtypeStruct(s, F32) f...]
    pallas_call x1 -> x0, local copies, waits for them, and re-layouts: 3.75 us -> none  [compute(): pl.pallas_call(compute_kernel, out_shape=jax.ShapeDtypeStruct((2, 19, 8,...]
    pallas_call x1, Pallas kernels: 19.1 us -> 17.8 us  [compute(): pl.pallas_call(compute_kernel, out_shape=jax.ShapeDtypeStruct((2, 19, 96,...]
where the time goes in v1:
time: 39.4 us; the launch traced here: 38.7 us
  Pallas kernels  36 us (91%)
  local copies, waits for them, and re-layouts  2.6 us (7%)
    pallas_call x1, Pallas kernels, exchange(): pl.pallas_call(exchange_kernel, out_shape=[jax.ShapeDtypeStruct(s, F32) f...  18.2 us
    pallas_call x1, Pallas kernels, compute(): pl.pallas_call(compute_kernel, out_shape=jax.ShapeDtypeStruct((2, 19, 96,...  17.8 us
    unnamed x6, local copies, waits for them, and re-layouts  2.6 us

profile of v1, /device:TPU:1, one launch (start us, length us, event | category | flops | bytes accessed | tf_op | source)
XLA Modules:
  0.0 38.7 jit_solution(17167314484306181715)
XLA Ops:
  0.0 0.0 copy-start
  0.0 0.9 %copy-done = f32[3,8,12,128]{3,1,2,0:T(8,128)S(1)} copy-done((f32[3,8,12,128]{3,1,2,0:T(8,128)S(1)}, f32[3,8,12,128]{3,1,2,0:T(8,128)}, u32[]{:S(2)}) %copy-start) | copy-done | bytes 147480
  0.9 0.0 copy-start.1
  0.9 0.9 %copy-done.1 = f32[2,8,12,128]{3,1,2,0:T(8,128)S(1)} copy-done((f32[2,8,12,128]{3,1,2,0:T(8,128)S(1)}, f32[2,8,12,128]{3,1,2,0:T(8,128)}, u32[]{:S(2)}) %copy-start.1) | copy-done | bytes 98328
  1.8 0.0 copy-start.2
  1.8 0.8 %copy-done.2 = s32[8,12,128]{2,0,1:T(8,128)S(1)} copy-done((s32[8,12,128]{2,0,1:T(8,128)S(1)}, s32[8,12,128]{2,0,1:T(8,128)}, u32[]{:S(2)}) %copy-start.2) | copy-done | bytes 49176
  2.6 18.2 %shard_map.37 = (f32[2,2,48,128]{3,2,1,0:T(8,128)S(1)}, f32[3,3,32,128]{3,2,1,0:T(8,128)S(1)}, f32[2,2,2,8,128]{4,3,2,1,0:T(8,128)S(1)}, f32[2,2,2,40,128]{4,3,2...) custom-call(s32[96,128]{1,0:T(8,128)S(1)} %bitcast.14, ...), custom_call_target="tpu_custom_call" | custom-call | tf_op jit(solution)/shard_map/pallas_call | solution.py:136
  20.9 17.8 %shard_map.38 = f32[2,19,96,128]{3,2,1,0:T(8,128)} custom-call(f32[2,2,48,128]{3,2,1,0:T(8,128)S(1)} %get-tuple-element.16.ro, f32[3,3,32,128]{3,2,1,0:T(8,128)S(1)} %get-tuple-element.17.uo, f32[2,2,2,8,128]{4,3,2,1,0:T(8,128)S(1)} %get-tuple-element.18.zp, f32[2,2,2,40,128]{4,3,2,1,0:T(8,128)S(1)} %get-tuple-element.19.rx, ...), custom_call_target="tpu_custom_call" | custom-call | tf_op jit(solution)/shard_map/pallas_call | solution.py:438
Async XLA Ops:
  0.0 0.9 %copy-start = (f32[3,8,12,128]{3,1,2,0:T(8,128)S(1)}, f32[3,8,12,128]{3,1,2,0:T(8,128)}, u32[]{:S(2)}) copy-start(f32[3,8,12,128]{3,1,2,0:T(8,128)} %param.5) | copy-start | bytes 442372
  0.9 0.9 %copy-start.1 = (f32[2,8,12,128]{3,1,2,0:T(8,128)S(1)}, f32[2,8,12,128]{3,1,2,0:T(8,128)}, u32[]{:S(2)}) copy-start(f32[2,8,12,128]{3,1,2,0:T(8,128)} %param.4) | copy-start | bytes 294916
  1.8 0.8 %copy-start.2 = (s32[8,12,128]{2,0,1:T(8,128)S(1)}, s32[8,12,128]{2,0,1:T(8,128)}, u32[]{:S(2)}) copy-start(s32[8,12,128]{2,0,1:T(8,128)} %param.3) | copy-start | bytes 147460

commit v2 on v1

--- a/solution.py
+++ b/solution.py
@@ -15,11 +15,14 @@
         (1, 0, -1), (-1, 0, 1), (0, 1, 1), (0, -1, -1), (0, 1, -1), (0, -1, 1)]
 TAU_INV = (1.0, 1.25)
 SRC = (0.5, 0.375)
+REACHES = ((1, 0.25, 0.125), (2, 0.5 / 6, 0.5 / 12))
 GROUPS = [(a, b) for a in (-1, 0, 1) for b in (-1, 0, 1)]
 ZGROUPS = [(0, 0), (1, 0), (-1, 0), (0, 1), (0, -1)]
 NEIGHBOURS = [d for d in itertools.product((-1, 0, 1), repeat=3) if d != (0, 0, 0)]
-EXCHANGED = [(2, 2, 48, 128), (3, 3, 32, 128), (2, 2, 2, 8, 128),
-             (2, 2, 2, 40, 128), (2, 3, 3, 16, 128),
+OWN = [(2, 2, 48, 128), (3, 3, 32, 128)]
+Z_PACK = (2, 2, 2, 8, 128)
+EXCHANGED = OWN + [
+    (2, 2, 2, 40, 128), (2, 3, 3, 16, 128),
              (2, 2, 48, 128), (2, 3, 32, 128),
              (2, 2, 2, 40, 128), (2, 2, 3, 16, 128),
              (2, 3, 2, 2, 8, 128), (2, 3, 2, 2, 8, 128)]
@@ -47,34 +50,41 @@
     return (0, 96 + 6 * x) if x < 4 else (1, 96 + 6 * (x - 4))
 
 
-def exchange_kernel(lab_ref, jit_ref, vel_ref, ro, uo, zp, rx, ux, ry, uy, re, ue, zf, ze,
-                    labv, jitv, velv, lsem, ssem, rsem, below):
+def exchange_kernel(lab_ref, jit_ref, vel_ref, ro_out, uo_out, rx, ux, ry, uy, re, ue, zf, ze,
+                    lab, rho, vel, ro, uo, zp, load_sem, store_sem, ssem, rsem, answer):
     ix, iy, iz = lax.axis_index("gx"), lax.axis_index("gy"), lax.axis_index("gz")
     nx, ny, nz = lax.axis_size("gx"), lax.axis_size("gy"), lax.axis_size("gz")
 
     def device(d):
         return (lax.rem(ix + d[0] + nx, nx), lax.rem(iy + d[1] + ny, ny), lax.rem(iz + d[2] + nz, nz))
 
+    place = lax.rem(iz, 8)
+    first_up, first_down = place != 7, place == 0
     barrier = pltpu.get_barrier_semaphore()
-    for d in NEIGHBOURS:
-        if d[2] <= 0:
-            pl.semaphore_signal(barrier, inc=1, device_id=device(d), device_id_type=MESH)
-    loads = [pltpu.make_async_copy(a, b, lsem.at[n]) for n, (a, b) in
-             enumerate(((lab_ref, labv), (jit_ref, jitv), (vel_ref, velv)))]
+
+    def tell(semaphore, dz):
+        for d in NEIGHBOURS:
+            if d[2] == dz:
+                pl.semaphore_signal(semaphore, inc=1, device_id=device(d), device_id_type=MESH)
+
+    tell(barrier, 0)
+    pl.when(first_up)(lambda: tell(barrier, 1))
+    pl.when(first_down)(lambda: tell(barrier, -1))
+    loads = [pltpu.make_async_copy(a, b, load_sem.at[n])
+             for n, (a, b) in enumerate(((lab_ref, lab), (jit_ref, rho), (vel_ref, vel)))]
     for load in loads:
         load.start()
     for load in loads:
         load.wait()
-    drop = labv[...] == 1
-    jitv[0] = jnp.where(drop, 2.0, 0.15).astype(F32) * jitv[0]
-    jitv[1] = jnp.where(drop, 0.15, 2.0).astype(F32) * jitv[1]
+    rho[0] = jnp.where(lab[...] == 1, 2.0, 0.15).astype(F32) * rho[0]
+    rho[1] = jnp.where(lab[...] == 1, 0.15, 2.0).astype(F32) * rho[1]
     lane = lane_of(6)
     for h in range(2):
         packs = [[jnp.zeros((6, 128), F32) for _ in range(2)] for _ in range(2)]
         for f in range(5):
             for x in range(8):
                 rows = pl.ds(48 * h + x, 6, stride=8)
-                val = jitv[f, rows, :] if f < 2 else velv[f - 2, rows, :]
+                val = rho[f, rows, :] if f < 2 else vel[f - 2, rows, :]
                 if f < 2:
                     ro[f, h, 6 * x:6 * x + 6, :] = val
                 k, l0 = z_place(f, x)
@@ -88,30 +98,43 @@
     for f in range(3):
         for g in range(3):
             for x in range(8):
-                uo[f, g, 4 * x:4 * x + 4, :] = velv[f, pl.ds(32 * g + x, 4, stride=8), :]
-    pl.semaphore_wait(barrier, 17)
-    for d in NEIGHBOURS:
-        if d[2] == 1:
-            pl.semaphore_signal(below, inc=1, device_id=device(d), device_id_type=MESH)
-
+                uo[f, g, 4 * x:4 * x + 4, :] = vel[f, pl.ds(32 * g + x, 4, stride=8), :]
+    pl.semaphore_wait(barrier, 8 + 9 * (place == 7).astype(jnp.int32) + 9 * (place != 0).astype(jnp.int32))
+    pl.when(jnp.logical_not(first_up))(lambda: tell(answer.at[1], 1))
+    pl.when(jnp.logical_not(first_down))(lambda: tell(answer.at[0], -1))
+
+    stores = [pltpu.make_async_copy(a, b, store_sem.at[n])
+              for n, (a, b) in enumerate(((ro, ro_out), (uo, uo_out)))]
     copies = []
 
-    def send(src, dst, d):
+    def plan(src, dst, d):
         n = len(copies)
         copy = pltpu.make_async_remote_copy(src_ref=src, dst_ref=dst, send_sem=ssem.at[n], recv_sem=rsem.at[n],
                                             device_id=device(d), device_id_type=MESH)
-        copy.start()
         copies.append(copy)
-
-    def send_z(dz):
+        return copy
+
+    def send(src, dst, d):
+        plan(src, dst, d).start()
+
+    def plan_z(dz):
         zs_mine, zs_theirs = (1, 0) if dz == 1 else (0, 1)
+        group = []
         for dx in (0, 1, -1):
-            send(zp.at[zs_mine], zf.at[zs_theirs, 1 - dx], (dx, 0, dz))
+            group.append(plan(zp.at[zs_mine], zf.at[zs_theirs, 1 - dx], (dx, 0, dz)))
             for dy in (1, -1):
                 h, side = (1, 0) if dy == 1 else (0, 1)
-                send(zp.at[zs_mine, h], ze.at[zs_theirs, 1 - dx, side], (dx, dy, dz))
-
-    send_z(1)
+                group.append(plan(zp.at[zs_mine, h], ze.at[zs_theirs, 1 - dx, side], (dx, dy, dz)))
+        return group
+
+    up, down = plan_z(1), plan_z(-1)
+
+    def start(group):
+        for copy in group:
+            copy.start()
+
+    pl.when(jnp.logical_not(first_up))(lambda: start(up))
+    pl.when(jnp.logical_not(first_down))(lambda: start(down))
     for dx in (1, -1):
         sx, r0, u0 = (0, 8, 16) if dx == 1 else (1, 0, 0)
         send(ro.at[:, :, r0:r0 + 40], rx.at[sx], (dx, 0, 0))
@@ -124,56 +147,76 @@
         sy, h, g = (0, 1, 2) if dy == 1 else (1, 0, 0)
         send(ro.at[:, h], ry.at[sy], (0, dy, 0))
         send(uo.at[:, g], uy.at[sy], (0, dy, 0))
-    pl.semaphore_wait(below, 9)
-    send_z(-1)
-    for copy in copies:
+
+    for store in stores:
+        store.start()
+
+    @pl.when(first_down)
+    def _():
+        pl.semaphore_wait(answer.at[1], 9)
+        start(down)
+
+    @pl.when(first_up)
+    def _():
+        pl.semaphore_wait(answer.at[0], 9)
+        start(up)
+
+    for copy in copies + stores:
         copy.wait()
 
 
 def exchange(labels, jitter, velocity):
-    hbm = pl.BlockSpec(memory_space=pltpu.HBM)
-    vmem = pl.BlockSpec(memory_space=pltpu.VMEM)
+    anywhere = pl.BlockSpec(memory_space=pl.ANY)
     return pl.pallas_call(
         exchange_kernel,
         out_shape=[jax.ShapeDtypeStruct(s, F32) for s in EXCHANGED],
-        in_specs=[hbm] * 3,
-        out_specs=[vmem] * len(EXCHANGED),
-        scratch_shapes=[pltpu.VMEM((96, 128), jnp.int32), pltpu.VMEM((2, 96, 128), F32),
-                        pltpu.VMEM((3, 96, 128), F32), pltpu.SemaphoreType.DMA((3,)),
-                        pltpu.SemaphoreType.DMA((34,)), pltpu.SemaphoreType.DMA((34,)), pltpu.SemaphoreType.REGULAR],
-        compiler_params=pltpu.CompilerParams(collective_id=0, has_side_effects=True, vmem_limit_bytes=8 << 20),
+        in_specs=[anywhere] * 3,
+        out_specs=[anywhere] * len(EXCHANGED),
+        scratch_shapes=[pltpu.VMEM((96, 128), jnp.int32), pltpu.VMEM((2, 96, 128), F32), pltpu.VMEM((3, 96, 128), F32)]
+        + [pltpu.VMEM(s, F32) for s in OWN + [Z_PACK]]
+        + [pltpu.SemaphoreType.DMA((3,)), pltpu.SemaphoreType.DMA((2,)), pltpu.SemaphoreType.DMA((34,)),
+           pltpu.SemaphoreType.DMA((34,)), pltpu.SemaphoreType.REGULAR((2,))],
+        compiler_params=pltpu.CompilerParams(collective_id=0, has_side_effects=True, vmem_limit_bytes=60 << 20),
     )(labels, jitter, velocity)
 
 
 NS1, NP1, NS2 = 34, 26, 28
 
 
-def stage_a(src, slab, rho_is, fields):
+def stage_z(src, slab, fp, fz, p0):
     for s in range(2):
         p = 1.0 - jnp.exp(-src[s, slab])
-        fields[s, 0, slab] = p
-        for n, (k, c6, c12) in enumerate(((1, 0.25, 0.125), (2, 0.5 / 6, 0.5 / 12))):
+        fp[s, slab, p0:p0 + 24] = p
+        for n, (k, c6, c12) in enumerate(REACHES):
             up, down = lroll(p, -k), lroll(p, k)
-            bz = c6 * p + c12 * (up + down)
-            dz = c12 * (up - down)
-            fields[s, 1 + n, slab] = bz + c12 * (yroll(p, k) + yroll(p, -k))
-            fields[s, 3 + n, slab] = bz
-            fields[s, 5 + n, slab] = 2.0 * dz + (yroll(dz, k) + yroll(dz, -k))
-            fields[s, 7 + n, slab] = dz
-
-
-def force(fields, slab, rows):
+            fz[s, n, 0, slab, p0:p0 + 24] = c6 * p + c12 * (up + down)
+            fz[s, n, 1, slab, p0:p0 + 24] = c12 * (up - down)
+
+
+def stage_y(slab, fp, fz, fy, rows):
+    for s in range(2):
+        for n, (k, c6, c12) in enumerate(REACHES):
+            p_up, p_down = fp[s, slab, 8 + k:8 + k + rows], fp[s, slab, 8 - k:8 - k + rows]
+            b_up, b_down = fz[s, n, 0, slab, 8 + k:8 + k + rows], fz[s, n, 0, slab, 8 - k:8 - k + rows]
+            d_up, d_down = fz[s, n, 1, slab, 8 + k:8 + k + rows], fz[s, n, 1, slab, 8 - k:8 - k + rows]
+            fy[s, n, 0, slab, 0:rows] = fz[s, n, 0, slab, 8:8 + rows] + c12 * (p_up + p_down)
+            fy[s, n, 1, slab, 0:rows] = b_up - b_down
+            fy[s, n, 2, slab, 0:rows] = c12 * (p_up - p_down)
+            fy[s, n, 3, slab, 0:rows] = 2.0 * fz[s, n, 1, slab, 8:8 + rows] + (d_up + d_down)
+
+
+def force(fp, fz, fy, slab, rows):
     near, far = [], []
     for s in range(2):
-        for n, (k, c12, out) in enumerate(((1, 0.125, near), (2, 0.5 / 12, far))):
-            gx = fields[s, 1 + n, slab + k, 0:rows] - fields[s, 1 + n, slab - k, 0:rows]
-            by = fields[s, 3 + n, slab] + c12 * (fields[s, 0, slab + k] + fields[s, 0, slab - k])
-            gy = (yroll(by, -k) - yroll(by, k))[0:rows]
-            gz = fields[s, 5 + n, slab, 0:rows] + (fields[s, 7 + n, slab + k, 0:rows] + fields[s, 7 + n, slab - k, 0:rows])
+        for n, out in enumerate((near, far)):
+            k = n + 1
+            gx = fy[s, n, 0, slab + k, 0:rows] - fy[s, n, 0, slab - k, 0:rows]
+            gy = fy[s, n, 1, slab, 0:rows] + (fy[s, n, 2, slab + k, 0:rows] + fy[s, n, 2, slab - k, 0:rows])
+            gz = fy[s, n, 3, slab, 0:rows] + (fz[s, n, 1, slab + k, 8:8 + rows] + fz[s, n, 1, slab - k, 8:8 + rows])
             out.append((gx, gy, gz))
     result = []
     for s in range(2):
-        minus = -fields[s, 0, slab, 0:rows]
+        minus = -fp[s, slab, 8:8 + rows]
         result.append([minus * (near[1 - s][a] + far[s][a]) for a in range(3)])
     return result
 
@@ -216,8 +259,18 @@
     return post
 
 
-def compute_kernel(ro, uo, zp, rx, ux, ry, uy, re, ue, zf, ze, out_ref,
-                   rho, vel, zr, fld, pops, qs, qz, rho1, mom, sout, outx, sem):
+def compute_kernel(*refs):
+    parts, out_ref, held, load_sem = refs[:10], refs[10], refs[11:21], refs[21]
+    loads = [pltpu.make_async_copy(a, b, load_sem.at[n]) for n, (a, b) in enumerate(zip(parts, held))]
+    for load in loads:
+        load.start()
+    for load in loads:
+        load.wait()
+    compute_parts(*held, out_ref, *refs[22:])
+
+
+def compute_parts(ro, uo, rx, ux, ry, uy, re, ue, zf, ze, out_ref,
+                  rho, vel, zr, fp, fz, fy, pops, qs, qz, rho1, mom, kept, sout, outx, sem):
     for e in range(20):
         dx, x = (0, e + 2) if e < 6 else (1, e - 6) if e < 14 else (2, e - 14)
         for c in range(2):
@@ -303,16 +356,20 @@
                 vel[f - 2, 16 + xo] = low
                 vel[f - 2, 19 + xo] = high
 
-    @pl.loop(0, NS1)
+    @pl.loop(0, NS1, unroll=17)
     def _(slab):
-        stage_a(rho, slab, None, fld)
-
-    @pl.loop(0, 22)
+        stage_z(rho, slab, fp, fz, 8)
+
+    @pl.loop(0, NS1, unroll=17)
+    def _(slab):
+        stage_y(slab, fp, fz, fy, 24)
+
+    @pl.loop(0, 22, unroll=2)
     def _(j):
         late, later = (j >= 16).astype(jnp.int32), (j >= 19).astype(jnp.int32)
         slab = j + 2 + 4 * late + 4 * later
         dst = j + late + 2 * later
-        fs = force(fld, slab, 24)
+        fs = force(fp, fz, fy, slab, 24)
         r = [rho[s, slab] for s in range(2)]
         u = [vel[a, j] for a in range(3)]
         half = 0.5 / (r[0] + r[1])
@@ -352,7 +409,7 @@
             if cx == -1:
                 pops[i, base + 4, 8:32] = lroll(pops[i, base + 1, 8:32], -18)
 
-    @pl.loop(0, 20)
+    @pl.loop(0, 20, unroll=4)
     def _(g):
         late, later = (g >= 14).astype(jnp.int32), (g >= 17).astype(jnp.int32)
         src = g + 1 + 2 * late + 2 * later
@@ -366,8 +423,8 @@
                 bottom = bottom + qs[s, n, src - cx, 5 - cy:13 - cy]
                 mx = mx + cx * a if cx else mx
                 my = my + cy * a if cy else my
-            rho1[s, dst, 0:16] = top
-            rho1[s, dst, 16:24] = bottom
+            rho1[s, dst, 8:24] = top
+            rho1[s, dst, 0:8] = bottom
         mz = 0.0
         for n, (cx, cy) in enumerate(ZGROUPS):
             mz = mz + qz[n, src - cx, 13 - cy:29 - cy]
@@ -380,74 +437,95 @@
             rho1[s, base + 5] = lroll(rho1[s, base + 2], -18)
             rho1[s, base + 6] = lroll(rho1[s, base + 3], -18)
 
-    @pl.loop(0, NS2)
+    @pl.loop(0, NS2, unroll=14)
     def _(slab):
-        stage_a(rho1, slab, None, fld)
-
-    def second(slab, src, write):
-        fs = force(fld, slab, 16)
-        r = [rho1[s, slab, 0:16] for s in range(2)]
-        inv = 1.0 / (r[0] + r[1])
-        v = [(mom[a, slab] + 0.5 * (fs[0][a] + fs[1][a])) * inv for a in range(3)]
-        for s in range(2):
-            post = populations(s, r[s], v, fs[s])
-            for i, (cx, cy, cz) in enumerate(VELS):
-                val = post[VELS[i]]
-                if s == 1:
-                    val = val - 0.25 * pops[i, src - cx, 13 - cy:29 - cy]
-                write(s, i, yroll(lroll(val, cz), cy - 1))
-
-    @pl.loop(0, 6)
+        stage_z(rho1, slab, fp, fz, 0)
+
+    @pl.loop(0, NS2, unroll=14)
+    def _(slab):
+        stage_y(slab, fp, fz, fy, 16)
+
+    def motion(slab):
+        fs = force(fp, fz, fy, slab, 16)
+        inv = 1.0 / (rho1[0, slab, 8:24] + rho1[1, slab, 8:24])
+        return [(mom[a, slab] + 0.5 * (fs[0][a] + fs[1][a])) * inv for a in range(3)], fs
+
+    def second(s, slab, src, v, f, write):
+        post = populations(s, rho1[s, slab, 8:24], v, f)
+        for i, (cx, cy, cz) in enumerate(VELS):
+            val = post[VELS[i]]
+            if s == 1:
+                val = val - 0.25 * pops[i, src - cx, 13 - cy:29 - cy]
+            write(i, yroll(lroll(val, cz), cy - 1))
+
+    @pl.loop(0, 6, unroll=2)
     def _(t):
         later = (t >= 3).astype(jnp.int32)
 
-        def write(s, i, val):
-            sout[s, i, t] = val
-
-        second(16 + t + 4 * later, 17 + t + 2 * later, write)
+        v, fs = motion(16 + t + 4 * later)
+        for s in range(2):
+            def write(i, val):
+                sout[s, i, t] = val
+
+            second(s, 16 + t + 4 * later, 17 + t + 2 * later, v, fs[s], write)
 
     lane16 = lane_of(16)
     seg16 = lane16 % 18
     from_low = (seg16 >= 6) & (seg16 < 12)
     edge = (lane16 < 6) | (lane16 >= 122)
 
-    @pl.loop(0, 10)
-    def _(k):
+    def finish(s, k, v, f):
         e = k + 5
         seg = e // 3
         xo = e - 3 * seg
         shift = lax.rem(256 - 18 * seg - 6, 128)
 
-        def write(s, i, val):
-            cx = VELS[i][0]
+        def write(i, val):
             strip = jnp.where(from_low, sout[s, i, xo], sout[s, i, xo + 3])
             val = jnp.where(edge, pltpu.roll(strip, shift, 1), val)
-            x = k - 1 + cx
-            inside = (x >= 0) & (x < 8)
-            outx[s, i, pl.ds(jnp.where(inside, x, 96), 12, stride=8)] = val[0:12]
-
-        second(k + 2, k + 3, write)
-
-    copy = pltpu.make_async_copy(outx.at[:, :, 0:96], out_ref, sem.at[0])
-    copy.start()
-    copy.wait()
+            x = k - 1 + VELS[i][0]
+            outx[s, i, pl.ds(jnp.where((x >= 0) & (x < 8), x, 96), 12, stride=8)] = val[0:12]
+
+        second(s, k + 2, k + 3, v, f, write)
+
+    @pl.loop(0, 10, unroll=2)
+    def _(k):
+        v, fs = motion(k + 2)
+        for a in range(3):
+            kept[a, k] = v[a]
+            kept[3 + a, k] = fs[1][a]
+        finish(0, k, v, fs[0])
+
+    first = pltpu.make_async_copy(outx.at[0, :, 0:96], out_ref.at[0], sem.at[0])
+    first.start()
+
+    @pl.loop(0, 10, unroll=2)
+    def _(k):
+        finish(1, k, [kept[a, k] for a in range(3)], [kept[3 + a, k] for a in range(3)])
+
+    second_half = pltpu.make_async_copy(outx.at[1, :, 0:96], out_ref.at[1], sem.at[1])
+    second_half.start()
+    first.wait()
+    second_half.wait()
 
 
 def compute(parts):
-    vmem = pl.BlockSpec(memory_space=pltpu.VMEM)
+    anywhere = pl.BlockSpec(memory_space=pl.ANY)
     return pl.pallas_call(
         compute_kernel,
         out_shape=jax.ShapeDtypeStruct((2, 19, 96, 128), F32),
-        in_specs=[vmem] * len(parts),
-        out_specs=pl.BlockSpec(memory_space=pltpu.HBM),
-        scratch_shapes=[
-            pltpu.VMEM((2, NS1, 24, 128), F32), pltpu.VMEM((3, 22, 24, 128), F32), pltpu.VMEM((2, 3, 2, 24, 128), F32),
-            pltpu.VMEM((2, 9, NS1, 24, 128), F32), pltpu.VMEM((19, NP1, 40, 128), F32),
+        in_specs=[anywhere] * len(parts),
+        out_specs=anywhere,
+        scratch_shapes=[pltpu.VMEM(part.shape, F32) for part in parts] + [
+            pltpu.SemaphoreType.DMA((len(parts),)), pltpu.VMEM((2, NS1, 24, 128), F32), pltpu.VMEM((3, 22, 24, 128), F32), pltpu.VMEM((2, 3, 2, 24, 128), F32),
+            pltpu.VMEM((2, NS1, 40, 128), F32), pltpu.VMEM((2, 2, 2, NS1, 40, 128), F32),
+            pltpu.VMEM((2, 2, 4, NS1, 24, 128), F32), pltpu.VMEM((19, NP1, 40, 128), F32),
             pltpu.VMEM((2, 9, NP1, 40, 128), F32), pltpu.VMEM((5, NP1, 40, 128), F32),
             pltpu.VMEM((2, NS2, 24, 128), F32), pltpu.VMEM((3, NS2, 16, 128), F32),
+            pltpu.VMEM((6, 10, 16, 128), F32),
             pltpu.VMEM((2, 19, 6, 16, 128), F32),
-            pltpu.VMEM((2, 19, 192, 128), F32), pltpu.SemaphoreType.DMA((1,))],
-        compiler_params=pltpu.CompilerParams(vmem_limit_bytes=40 << 20),
+            pltpu.VMEM((2, 19, 192, 128), F32), pltpu.SemaphoreType.DMA((2,))],
+        compiler_params=pltpu.CompilerParams(vmem_limit_bytes=60 << 20),
     )(*parts)
 
 

time: 39.4 us -> 33.1 us (0.84)
  the two profiles are of different devices: /device:TPU:1 before, /device:TPU:33 now
where the time goes in v2:
time: 33.1 us; the launch traced here: 33 us
  Pallas kernels  33 us (100%)
    pallas_call x1, Pallas kernels, exchange(): pl.pallas_call(exchange_kernel, out_shape=[jax.ShapeDtypeStruct(s, F32) f...  18.9 us
    pallas_call x1, Pallas kernels, compute(): pl.pallas_call(compute_kernel, out_shape=jax.ShapeDtypeStruct((2, 19, 96,...  14.1 us

profile of v2, /device:TPU:33, one launch (start us, length us, event | category | flops | bytes accessed | tf_op | source)
XLA Modules:
  0.0 33.0 jit_solution(8098537607637496103)
XLA Ops:
  0.0 18.9 %shard_map.37 = (f32[2,2,48,128]{3,2,1,0:T(8,128)}, f32[3,3,32,128]{3,2,1,0:T(8,128)}, f32[2,2,2,40,128]{4,3,2,1,0:T(8,128)}, f32[2,3,3,16,128]{4,3,2,1,0:T(8,12...) custom-call(s32[96,128]{1,0:T(8,128)} %bitcast.14, ...), custom_call_target="tpu_custom_call" | custom-call | tf_op jit(solution)/shard_map/pallas_call | solution.py:170
  18.9 14.1 %shard_map.38 = f32[2,19,96,128]{3,2,1,0:T(8,128)} custom-call(f32[2,2,48,128]{3,2,1,0:T(8,128)} %get-tuple-element.15.refs_0_, f32[3,3,32,128]{3,2,1,0:T(8,128)} %get-tuple-element.16.refs_1_, f32[2,2,2,40,128]{4,3,2,1,0:T(8,128)} %get-tuple-element.17.refs_2_, f32[2,3,3,16,128]{4,3,2,1,0:T(8,128)} %get-tuple-element.18.refs_3_, ...), custom_call_target="tpu_custom_call" | custom-call | tf_op jit(solution)/shard_map/pallas_call | solution.py:514

commit v3 on v2

--- a/solution.py
+++ b/solution.py
@@ -151,15 +151,15 @@
     for store in stores:
         store.start()
 
+    @pl.when(first_up)
+    def _():
+        pl.semaphore_wait(answer.at[0], 9)
+        start(up)
+
     @pl.when(first_down)
     def _():
         pl.semaphore_wait(answer.at[1], 9)
         start(down)
-
-    @pl.when(first_up)
-    def _():
-        pl.semaphore_wait(answer.at[0], 9)
-        start(up)
 
     for copy in copies + stores:
         copy.wait()
@@ -205,18 +205,19 @@
             fy[s, n, 3, slab, 0:rows] = 2.0 * fz[s, n, 1, slab, 8:8 + rows] + (d_up + d_down)
 
 
-def force(fp, fz, fy, slab, rows):
+def force(fp, fz, fy, slab, r0, rows):
+    here, inner = pl.ds(r0, rows), pl.ds(r0 + 8, rows)
     near, far = [], []
     for s in range(2):
         for n, out in enumerate((near, far)):
             k = n + 1
-            gx = fy[s, n, 0, slab + k, 0:rows] - fy[s, n, 0, slab - k, 0:rows]
-            gy = fy[s, n, 1, slab, 0:rows] + (fy[s, n, 2, slab + k, 0:rows] + fy[s, n, 2, slab - k, 0:rows])
-            gz = fy[s, n, 3, slab, 0:rows] + (fz[s, n, 1, slab + k, 8:8 + rows] + fz[s, n, 1, slab - k, 8:8 + rows])
+            gx = fy[s, n, 0, slab + k, here] - fy[s, n, 0, slab - k, here]
+            gy = fy[s, n, 1, slab, here] + (fy[s, n, 2, slab + k, here] + fy[s, n, 2, slab - k, here])
+            gz = fy[s, n, 3, slab, here] + (fz[s, n, 1, slab + k, inner] + fz[s, n, 1, slab - k, inner])
             out.append((gx, gy, gz))
     result = []
     for s in range(2):
-        minus = -fp[s, slab, 8:8 + rows]
+        minus = -fp[s, slab, inner]
         result.append([minus * (near[1 - s][a] + far[s][a]) for a in range(3)])
     return result
 
@@ -356,22 +357,25 @@
                 vel[f - 2, 16 + xo] = low
                 vel[f - 2, 19 + xo] = high
 
-    @pl.loop(0, NS1, unroll=17)
+    @pl.loop(0, NS1, unroll=34)
     def _(slab):
         stage_z(rho, slab, fp, fz, 8)
 
-    @pl.loop(0, NS1, unroll=17)
+    @pl.loop(0, NS1, unroll=34)
     def _(slab):
         stage_y(slab, fp, fz, fy, 24)
 
-    @pl.loop(0, 22, unroll=2)
-    def _(j):
+    @pl.loop(0, 66, unroll=66)
+    def _(i):
+        j = i // 3
+        r0 = pl.multiple_of(8 * (i - 3 * j), 8)
+        here, inner = pl.ds(r0, 8), pl.ds(r0 + 8, 8)
         late, later = (j >= 16).astype(jnp.int32), (j >= 19).astype(jnp.int32)
         slab = j + 2 + 4 * late + 4 * later
         dst = j + late + 2 * later
-        fs = force(fp, fz, fy, slab, 24)
-        r = [rho[s, slab] for s in range(2)]
-        u = [vel[a, j] for a in range(3)]
+        fs = force(fp, fz, fy, slab, r0, 8)
+        r = [rho[s, slab, here] for s in range(2)]
+        u = [vel[a, j, here] for a in range(3)]
         half = 0.5 / (r[0] + r[1])
         v = [u[a] + half * (fs[0][a] + fs[1][a]) for a in range(3)]
         zsum = {}
@@ -381,15 +385,15 @@
             for i, (cx, cy, cz) in enumerate(VELS):
                 val = lroll(post[VELS[i]], cz)
                 if s == 1:
-                    pops[i, dst, 8:32] = val
+                    pops[i, dst, inner] = val
                 sums[cx, cy] = val if (cx, cy) not in sums else sums[cx, cy] + val
                 if cz:
                     part = val if cz == 1 else -val
                     zsum[cx, cy] = part if (cx, cy) not in zsum else zsum[cx, cy] + part
             for n, key in enumerate(GROUPS):
-                qs[s, n, dst, 8:32] = sums[key]
+                qs[s, n, dst, inner] = sums[key]
         for n, key in enumerate(ZGROUPS):
-            qz[n, dst, 8:32] = zsum[key]
+            qz[n, dst, inner] = zsum[key]
 
     for base in (16, 21):
         for n, (cx, cy) in enumerate(GROUPS):
@@ -409,7 +413,7 @@
             if cx == -1:
                 pops[i, base + 4, 8:32] = lroll(pops[i, base + 1, 8:32], -18)
 
-    @pl.loop(0, 20, unroll=4)
+    @pl.loop(0, 20, unroll=20)
     def _(g):
         late, later = (g >= 14).astype(jnp.int32), (g >= 17).astype(jnp.int32)
         src = g + 1 + 2 * late + 2 * later
@@ -437,73 +441,77 @@
             rho1[s, base + 5] = lroll(rho1[s, base + 2], -18)
             rho1[s, base + 6] = lroll(rho1[s, base + 3], -18)
 
-    @pl.loop(0, NS2, unroll=14)
+    @pl.loop(0, NS2, unroll=28)
     def _(slab):
         stage_z(rho1, slab, fp, fz, 0)
 
-    @pl.loop(0, NS2, unroll=14)
+    @pl.loop(0, NS2, unroll=28)
     def _(slab):
         stage_y(slab, fp, fz, fy, 16)
 
-    def motion(slab):
-        fs = force(fp, fz, fy, slab, 16)
-        inv = 1.0 / (rho1[0, slab, 8:24] + rho1[1, slab, 8:24])
-        return [(mom[a, slab] + 0.5 * (fs[0][a] + fs[1][a])) * inv for a in range(3)], fs
-
-    def second(s, slab, src, v, f, write):
-        post = populations(s, rho1[s, slab, 8:24], v, f)
+    def motion(slab, r0):
+        here, inner = pl.ds(r0, 8), pl.ds(r0 + 8, 8)
+        fs = force(fp, fz, fy, slab, r0, 8)
+        inv = 1.0 / (rho1[0, slab, inner] + rho1[1, slab, inner])
+        return [(mom[a, slab, here] + 0.5 * (fs[0][a] + fs[1][a])) * inv for a in range(3)], fs
+
+    def second(s, slab, src, r0, v, f, write):
+        post = populations(s, rho1[s, slab, pl.ds(r0 + 8, 8)], v, f)
         for i, (cx, cy, cz) in enumerate(VELS):
             val = post[VELS[i]]
             if s == 1:
-                val = val - 0.25 * pops[i, src - cx, 13 - cy:29 - cy]
-            write(i, yroll(lroll(val, cz), cy - 1))
-
-    @pl.loop(0, 6, unroll=2)
+                val = val - 0.25 * pops[i, src - cx, pl.ds(r0 + 13 - cy, 8)]
+            write(i, lroll(val, cz))
+
+    @pl.loop(0, 6, unroll=6)
     def _(t):
         later = (t >= 3).astype(jnp.int32)
-
-        v, fs = motion(16 + t + 4 * later)
-        for s in range(2):
-            def write(i, val):
-                sout[s, i, t] = val
-
-            second(s, 16 + t + 4 * later, 17 + t + 2 * later, v, fs[s], write)
-
-    lane16 = lane_of(16)
-    seg16 = lane16 % 18
-    from_low = (seg16 >= 6) & (seg16 < 12)
-    edge = (lane16 < 6) | (lane16 >= 122)
-
-    def finish(s, k, v, f):
+        for r0 in (0, 8):
+            v, fs = motion(16 + t + 4 * later, r0)
+            for s in range(2):
+                def write(i, val):
+                    sout[s, i, t, r0:r0 + 8] = val
+
+                second(s, 16 + t + 4 * later, 17 + t + 2 * later, r0, v, fs[s], write)
+
+    lane8 = lane_of(8)
+    seg8 = lane8 % 18
+    from_low = (seg8 >= 6) & (seg8 < 12)
+    edge = (lane8 < 6) | (lane8 >= 122)
+
+    def finish(s, k, r0, v, f):
         e = k + 5
         seg = e // 3
         xo = e - 3 * seg
         shift = lax.rem(256 - 18 * seg - 6, 128)
 
         def write(i, val):
-            strip = jnp.where(from_low, sout[s, i, xo], sout[s, i, xo + 3])
+            strip = jnp.where(from_low, sout[s, i, xo, r0:r0 + 8], sout[s, i, xo + 3, r0:r0 + 8])
             val = jnp.where(edge, pltpu.roll(strip, shift, 1), val)
             x = k - 1 + VELS[i][0]
-            outx[s, i, pl.ds(jnp.where((x >= 0) & (x < 8), x, 96), 12, stride=8)] = val[0:12]
-
-        second(s, k + 2, k + 3, v, f, write)
-
-    @pl.loop(0, 10, unroll=2)
+            first = jnp.where((x >= 0) & (x < 8), 8 * (VELS[i][1] + 1) + x, 144)
+            outx[s, i, pl.ds(first + 8 * r0, 8, stride=8)] = val
+
+        second(s, k + 2, k + 3, r0, v, f, write)
+
+    @pl.loop(0, 10, unroll=10)
     def _(k):
-        v, fs = motion(k + 2)
-        for a in range(3):
-            kept[a, k] = v[a]
-            kept[3 + a, k] = fs[1][a]
-        finish(0, k, v, fs[0])
-
-    first = pltpu.make_async_copy(outx.at[0, :, 0:96], out_ref.at[0], sem.at[0])
+        for r0 in (0, 8):
+            v, fs = motion(k + 2, r0)
+            for a in range(3):
+                kept[a, k, r0:r0 + 8] = v[a]
+                kept[3 + a, k, r0:r0 + 8] = fs[1][a]
+            finish(0, k, r0, v, fs[0])
+
+    first = pltpu.make_async_copy(outx.at[0, :, 16:112], out_ref.at[0], sem.at[0])
     first.start()
 
-    @pl.loop(0, 10, unroll=2)
+    @pl.loop(0, 10, unroll=10)
     def _(k):
-        finish(1, k, [kept[a, k] for a in range(3)], [kept[3 + a, k] for a in range(3)])
-
-    second_half = pltpu.make_async_copy(outx.at[1, :, 0:96], out_ref.at[1], sem.at[1])
+        for r0 in (0, 8):
+            finish(1, k, r0, [kept[a, k, r0:r0 + 8] for a in range(3)], [kept[3 + a, k, r0:r0 + 8] for a in range(3)])
+
+    second_half = pltpu.make_async_copy(outx.at[1, :, 16:112], out_ref.at[1], sem.at[1])
     second_half.start()
     first.wait()
     second_half.wait()
@@ -524,7 +532,7 @@
             pltpu.VMEM((2, NS2, 24, 128), F32), pltpu.VMEM((3, NS2, 16, 128), F32),
             pltpu.VMEM((6, 10, 16, 128), F32),
             pltpu.VMEM((2, 19, 6, 16, 128), F32),
-            pltpu.VMEM((2, 19, 192, 128), F32), pltpu.SemaphoreType.DMA((2,))],
+            pltpu.VMEM((2, 19, 272, 128), F32), pltpu.SemaphoreType.DMA((2,))],
         compiler_params=pltpu.CompilerParams(vmem_limit_bytes=60 << 20),
     )(*parts)
 

time: 33.1 us -> 27.4 us (0.83)
  the two profiles are of different devices: /device:TPU:33 before, /device:TPU:1 now
where the time goes in v3:
time: 27.4 us; the launch traced here: 27.3 us
  Pallas kernels  27.3 us (100%)
    pallas_call x1, Pallas kernels, exchange(): pl.pallas_call(exchange_kernel, out_shape=[jax.ShapeDtypeStruct(s, F32) f...  17.2 us
    pallas_call x1, Pallas kernels, compute(): pl.pallas_call(compute_kernel, out_shape=jax.ShapeDtypeStruct((2, 19, 96,...  10.1 us

profile of v3, /device:TPU:1, one launch (start us, length us, event | category | flops | bytes accessed | tf_op | source)
XLA Modules:
  0.0 27.3 jit_solution(10323862872273783921)
XLA Ops:
  0.0 17.2 %shard_map.37 = (f32[2,2,48,128]{3,2,1,0:T(8,128)}, f32[3,3,32,128]{3,2,1,0:T(8,128)}, f32[2,2,2,40,128]{4,3,2,1,0:T(8,128)}, f32[2,3,3,16,128]{4,3,2,1,0:T(8,12...) custom-call(s32[96,128]{1,0:T(8,128)} %bitcast.14, ...), custom_call_target="tpu_custom_call" | custom-call | tf_op jit(solution)/shard_map/pallas_call | solution.py:170
  17.2 10.1 %shard_map.38 = f32[2,19,96,128]{3,2,1,0:T(8,128)} custom-call(f32[2,2,48,128]{3,2,1,0:T(8,128)} %get-tuple-element.15.refs_0_, f32[3,3,32,128]{3,2,1,0:T(8,128)} %get-tuple-element.16.refs_1_, f32[2,2,2,40,128]{4,3,2,1,0:T(8,128)} %get-tuple-element.17.refs_2_, f32[2,3,3,16,128]{4,3,2,1,0:T(8,128)} %get-tuple-element.18.refs_3_, ...), custom_call_target="tpu_custom_call" | custom-call | tf_op jit(solution)/shard_map/pallas_call | solution.py:522
